TPU v7x, 128 devices: a whole 4x4x4 slice. The times are simulated.
128 devices in a mesh: src: 4 (over x), grp: 32 (over z, y, core).
Axes of the slice: x: 4, y: 4, z: 4, core: 2. Of those that a mesh axis runs over, the one named last changes fastest.
Arguments:
- source_points: bfloat16 [32768, 64], P('src'), may hold values from -6 to 6
- source_logmass: float32 [32768], P('src'), may hold values from -1 to 1
- target_points: bfloat16 [524288, 64], P(('src', 'grp')), may hold values from -1.796875 to 1.796875
- target_logmass: float32 [524288], P(('src', 'grp')), may hold values from -1 to 1
- target_potential: float32 [524288], P(('src', 'grp')), may hold values from -1.5 to 61.5
- tile_slot: int32 [256, 256], P('src', 'grp'), may hold values from 0 to 31, as said below
- tile_counts: int32 [256, 32], P('src', 'grp'), may hold values from 2 to 8
- fetch_ids: int32 [16, 256], P('src', 'grp'), may hold values from 0 to 31, as said below
Outputs:
- source_field: float32 [32768], P('src')
- target_field: float32 [524288], P(('src', 'grp'))
Inputs may be any that keep to these rules, and one draw needn't show every extreme that they name: `tile_slot`: within one source block and group the live slots name distinct entries; every entry 0 to 31 of a device's fetch list is named by some live slot of that device. `fetch_ids`: each device names 8 distinct blocks of each peer in its group; every target block is named by some device of its group.
All inputs are finite; a program needn't handle non-finite values.
Results may differ from a plain program's by a relative error of at most 0.0003.
Values may be sent and summed in bfloat16 or wider, within the bound.
No kernel may reach another device: no remote copies, remote signals or barrier semaphores. Data moves between devices by JAX's collectives and lax.ppermute only.
A program may use at most 64 MiB of HBM per device.

v0:
```python
import math

import jax
import jax.numpy as jnp
from jax import lax
from jax.sharding import PartitionSpec as P

D = 64
BLOCK = 128
KG = 8
ITERS = 3


EPSILON = 0.25
LOWEST = -1e30


def shards(
    source_points,
    source_logmass,
    target_points,
    target_logmass,
    target_potential,
    tile_slot,
    tile_counts,
    fetch_ids,
):
    peers = lax.axis_size("src")
    blocks = tile_counts.shape[0]
    per_peer = fetch_ids.shape[1]
    owned = target_potential.shape[0] // BLOCK
    fetched_count = peers * per_peer
    requested = lax.all_to_all(fetch_ids, "src", split_axis=0, concat_axis=0, tiled=True)
    target_rows = target_points.reshape(owned, BLOCK * D)
    fetched = lax.all_to_all(
        target_rows[requested], "src", split_axis=0, concat_axis=0, tiled=True
    ).reshape(fetched_count, BLOCK, D)
    target_sq = jnp.sum(jnp.square(fetched.astype(jnp.float32)), -1)
    per_turn = math.gcd(blocks, max(1, 512 // BLOCK))
    turns = blocks // per_turn
    points = source_points.reshape(turns, per_turn, BLOCK, D)
    source_sq = jnp.sum(jnp.square(source_points.astype(jnp.float32)), -1).reshape(
        turns, per_turn, BLOCK
    )
    alive_mask = (jnp.arange(KG, dtype=jnp.int32)[None, :] < tile_counts).reshape(
        turns, per_turn, KG
    )
    slot_ids = tile_slot.reshape(turns, per_turn, KG)
    flat_slots = tile_slot.reshape(-1)

    def tile_cost(block_points, block_sq, block_slots):
        others = fetched[block_slots]
        products = jnp.einsum(
            "bid,bkjd->bkij", block_points, others, preferred_element_type=jnp.float32
        )
        return 0.5 * (block_sq[:, None, :, None] + target_sq[block_slots][:, :, None, :]) - products

    owned_pot = target_potential.reshape(owned, BLOCK)
    owned_mass = target_logmass.reshape(owned, BLOCK)
    flat_requested = requested.reshape(-1)
    for sweep_index in range(ITERS):
        pot_table = lax.all_to_all(
            owned_pot[requested], "src", split_axis=0, concat_axis=0, tiled=True
        ).reshape(fetched_count, BLOCK)

        def row_turn(turn_input):
            block_points, block_sq, block_slots, block_alive = turn_input
            scores = jnp.where(
                block_alive[:, :, None, None],
                (
                    pot_table[block_slots][:, :, None, :]
                    - tile_cost(block_points, block_sq, block_slots)
                )
                / EPSILON,
                LOWEST,
            )
            row_top = jnp.max(scores, axis=(1, 3))
            return (row_top, jnp.sum(jnp.exp(scores - row_top[:, None, :, None]), axis=(1, 3)))

        row_top, row_mass = lax.map(row_turn, (points, source_sq, slot_ids, alive_mask))
        row_top = row_top.reshape(-1)
        row_mass = row_mass.reshape(-1)
        highest = lax.pmax(row_top.astype(jnp.bfloat16), "grp").astype(row_top.dtype)
        row_mass = lax.psum(
            (row_mass * jnp.exp(row_top - highest)).astype(jnp.bfloat16), "grp"
        ).astype(jnp.float32)
        row_top = highest
        source_field = EPSILON * source_logmass - EPSILON * (row_top + jnp.log(row_mass))
        field_turns = source_field.reshape(turns, per_turn, BLOCK)

        def column_turn(turn_input):
            block_points, block_sq, block_slots, block_alive, block_field = turn_input
            scores = jnp.where(
                block_alive[:, :, None, None],
                (block_field[:, None, :, None] - tile_cost(block_points, block_sq, block_slots))
                / EPSILON,
                LOWEST,
            )
            col_top = jnp.max(scores, axis=2)
            col_mass = jnp.sum(jnp.exp(scores - col_top[:, :, None, :]), axis=2)
            return (col_top, jnp.where(block_alive[:, :, None], col_mass, 0.0))

        col_top, col_mass = lax.map(
            column_turn, (points, source_sq, slot_ids, alive_mask, field_turns)
        )
        col_top = col_top.reshape(-1, BLOCK)
        col_mass = col_mass.reshape(-1, BLOCK)
        slot_peak = (
            jnp.full((fetched_count, BLOCK), LOWEST, jnp.float32).at[flat_slots].max(col_top)
        )
        slot_mass = (
            jnp.zeros((fetched_count, BLOCK), jnp.float32)
            .at[flat_slots]
            .add(col_mass * jnp.exp(col_top - slot_peak[flat_slots]))
        )
        slot_peak, slot_mass = (slot_peak, slot_mass)
        back_peak, back_mass = (
            lax.all_to_all(
                slot_peak.reshape(peers, per_peer, BLOCK),
                "src",
                split_axis=0,
                concat_axis=0,
                tiled=True,
            ),
            lax.all_to_all(
                slot_mass.reshape(peers, per_peer, BLOCK),
                "src",
                split_axis=0,
                concat_axis=0,
                tiled=True,
            ),
        )
        back_peak = back_peak.reshape(-1, BLOCK)
        back_mass = back_mass.reshape(-1, BLOCK)
        col_peak = jnp.full((owned, BLOCK), LOWEST, jnp.float32).at[flat_requested].max(back_peak)
        col_total = (
            jnp.zeros((owned, BLOCK), jnp.float32)
            .at[flat_requested]
            .add(back_mass * jnp.exp(back_peak - col_peak[flat_requested]))
        )
        owned_pot = EPSILON * owned_mass - EPSILON * (col_peak + jnp.log(col_total))
    target_field = owned_pot.reshape(-1)
    return (source_field, target_field)


def solution(mesh):
    return jax.shard_map(
        shards,
        mesh=mesh,
        in_specs=(
            P("src", None),
            P("src"),
            P(("src", "grp"), None),
            P(("src", "grp")),
            P(("src", "grp")),
            P("src", "grp"),
            P("src", "grp"),
            P("src", "grp"),
        ),
        out_specs=(P("src"), P(("src", "grp"))),
        check_vma=False,
    )
```

profile of v0, /device:TPU:0, one launch (start us, length us, event | category | flops | bytes accessed | tf_op | source)
XLA Modules:
  0.0 1280.1 jit_solution(2276547273101056908)
XLA Ops:
  0.7 4.5 all-to-all-start
  13.5 4.8 all-to-all-start.2
  20.5 6.7 all-to-all-done.2
  27.2 3.3 all-to-all-start.1
  32.2 3.6 all-to-all-done.1
  35.8 79.9 %while.72 = (s32[]{:T(128)}, f32[16,4,128]{2,1,0:T(4,128)S(1)}, f32[16,4,128]{2,1,0:T(4,128)S(1)}, pred[16,4,8]{2,1,0:T(4,128)(4,1)S(1)}, s32[16,4,8]{2,1,0:T(4,...) while((s32[]{:T(128)}, f32[16,4,128]{2,1,0:T(4,128)S(1)}, ...), condition=%wide.region_5.6_spmd, body=%wide.region_2.5_spmd.sunk | while | flops 71827552 | bytes 5957341 | solution.py:80
  57.8 2.6 fusion.120
  82.8 2.6 fusion.120
  87.8 2.6 fusion.120
  115.7 126.5 %pmax.21 = bf16[8192]{0:T(1024)(128)(2,1)S(1)} all-reduce(bf16[8192]{0:T(1024)(128)(2,1)S(1)} %convert_element_type.44), channel_id=1, replica_groups=mesh['src'=4,'grp'=32] {'grp'}, use_global_device_ids=true, to_apply=%region_6.7 | all-reduce | flops 8192 | bytes 32768 | tf_op jit(solution)/shard_map/pmax | solution.py:83
  242.2 123.8 %psum.21 = bf16[8192]{0:T(1024)(128)(2,1)S(1)} all-reduce(bf16[8192]{0:T(1024)(128)(2,1)S(1)} %fusion.41), channel_id=1, replica_groups=mesh['src'=4,'grp'=32] {'grp'}, use_global_device_ids=true, to_apply=%region_7.8 | all-reduce | flops 8192 | bytes 32768 | tf_op jit(solution)/shard_map/psum | solution.py:84
  366.1 56.8 %while.73 = (s32[]{:T(128)}, f32[16,4,8,128]{3,2,1,0:T(8,128)S(1)}, f32[16,4,8,128]{3,2,1,0:T(8,128)S(1)}, pred[16,4,8]{2,1,0:T(4,128)(4,1)S(1)}, f32[16,4,128]{...) while((s32[]{:T(128)}, f32[16,4,8,128]{3,2,1,0:T(8,128)S(1)}, ...), condition=%wide.region_11.12_spmd, body=%wide.region_8.11_spmd.sunk | while | flops 71824480 | bytes 6015073 | solution.py:103
  423.0 2.8 scatter_custom_fusion
  427.5 3.4 all-to-all-start.3
  431.1 2.8 scatter_custom_fusion.2
  436.1 3.3 all-to-all-start.4
  440.1 4.6 all-to-all-done.4
  446.8 3.3 all-to-all-start.5
  450.0 5.3 all-to-all-done.5
  455.4 79.9 %while.74 = (s32[]{:T(128)}, f32[16,4,128]{2,1,0:T(4,128)S(1)}, f32[16,4,128]{2,1,0:T(4,128)S(1)}, pred[16,4,8]{2,1,0:T(4,128)(4,1)S(1)}, s32[16,4,8]{2,1,0:T(4,...) while((s32[]{:T(128)}, f32[16,4,128]{2,1,0:T(4,128)S(1)}, ...), condition=%wide.region_19.20_spmd, body=%wide.region_16.19_spmd.sunk | while | flops 71827552 | bytes 5957341 | solution.py:80
  462.4 2.6 fusion.125
  467.4 2.6 fusion.125
  477.4 2.6 fusion.125
  482.4 2.6 fusion.125
  502.4 2.6 fusion.125
  535.3 123.8 %pmax.22 = bf16[8192]{0:T(1024)(128)(2,1)S(1)} all-reduce(bf16[8192]{0:T(1024)(128)(2,1)S(1)} %convert_element_type.48), channel_id=1, replica_groups=mesh['src'=4,'grp'=32] {'grp'}, use_global_device_ids=true, to_apply=%region_20.21 | all-reduce | flops 8192 | bytes 32768 | tf_op jit(solution)/shard_map/pmax | solution.py:83
  659.1 123.8 %psum.22 = bf16[8192]{0:T(1024)(128)(2,1)S(1)} all-reduce(bf16[8192]{0:T(1024)(128)(2,1)S(1)} %fusion.46), channel_id=1, replica_groups=mesh['src'=4,'grp'=32] {'grp'}, use_global_device_ids=true, to_apply=%region_21.22 | all-reduce | flops 8192 | bytes 32768 | tf_op jit(solution)/shard_map/psum | solution.py:84
  783.0 57.1 %while.75 = (s32[]{:T(128)}, f32[16,4,8,128]{3,2,1,0:T(8,128)S(1)}, f32[16,4,8,128]{3,2,1,0:T(8,128)S(1)}, pred[16,4,8]{2,1,0:T(4,128)(4,1)S(1)}, f32[16,4,128]{...) while((s32[]{:T(128)}, f32[16,4,8,128]{3,2,1,0:T(8,128)S(1)}, ...), condition=%wide.region_25.26_spmd, body=%wide.region_22.25_spmd.sunk | while | flops 71824480 | bytes 6015073 | solution.py:103
  840.1 2.8 scatter_custom_fusion.4
  844.7 3.3 all-to-all-start.6
  848.0 2.8 scatter_custom_fusion.6
  853.3 3.3 all-to-all-start.7
  857.3 4.6 all-to-all-done.7
  863.9 3.3 all-to-all-start.8
  867.2 5.3 all-to-all-done.8
  872.5 79.9 %while.76 = (s32[]{:T(128)}, f32[16,4,128]{2,1,0:T(4,128)S(1)}, f32[16,4,128]{2,1,0:T(4,128)S(1)}, pred[16,4,8]{2,1,0:T(4,128)(4,1)S(1)}, s32[16,4,8]{2,1,0:T(4,...) while((s32[]{:T(128)}, f32[16,4,128]{2,1,0:T(4,128)S(1)}, ...), condition=%wide.region_33.34_spmd, body=%wide.region_30.33_spmd.sunk | while | flops 71827552 | bytes 5957341 | solution.py:80
  879.6 2.6 fusion.130
  894.5 2.6 fusion.130
  924.5 2.6 fusion.130
  929.5 2.6 fusion.130
  952.4 123.8 %pmax.23 = bf16[8192]{0:T(1024)(128)(2,1)S(1)} all-reduce(bf16[8192]{0:T(1024)(128)(2,1)S(1)} %convert_element_type.52), channel_id=1, replica_groups=mesh['src'=4,'grp'=32] {'grp'}, use_global_device_ids=true, to_apply=%region_34.35 | all-reduce | flops 8192 | bytes 32768 | tf_op jit(solution)/shard_map/pmax | solution.py:83
  1076.3 124.0 %psum.23 = bf16[8192]{0:T(1024)(128)(2,1)S(1)} all-reduce(bf16[8192]{0:T(1024)(128)(2,1)S(1)} %fusion.51), channel_id=1, replica_groups=mesh['src'=4,'grp'=32] {'grp'}, use_global_device_ids=true, to_apply=%region_35.36 | all-reduce | flops 8192 | bytes 32768 | tf_op jit(solution)/shard_map/psum | solution.py:84
  1200.4 56.5 %while.77 = (s32[]{:T(128)}, f32[16,4,8,128]{3,2,1,0:T(8,128)S(1)}, f32[16,4,8,128]{3,2,1,0:T(8,128)S(1)}, pred[16,4,8]{2,1,0:T(4,128)(4,1)S(1)}, f32[16,4,128]{...) while((s32[]{:T(128)}, f32[16,4,8,128]{3,2,1,0:T(8,128)S(1)}, ...), condition=%wide.region_39.40_spmd, body=%wide.region_36.39_spmd.sunk | while | flops 71824480 | bytes 6015073 | solution.py:103
  1256.9 2.8 scatter_custom_fusion.8
  1261.5 3.3 all-to-all-start.9
  1264.8 2.8 scatter_custom_fusion.10
  1270.1 3.2 all-to-all-start.10
  1274.0 4.6 all-to-all-done.10
  (1124 shorter events, 406.2 us)
Async XLA Ops:
  0.6 17.9 %copy-start = (f32[4096]{0:T(1024)S(1)}, f32[4096]{0:T(1024)}, u32[]{:S(2)}) copy-start(f32[4096]{0:T(1024)} %param.24) | copy-start | bytes 49156
  0.6 7.5 copy-start.6
  0.7 8.4 copy-start.5
  0.7 8.5 copy-start.1
  0.7 11.0 all-to-all-start
  13.5 13.7 %all-to-all-start.2 = ((bf16[4,8,8192]{2,1,0:T(8,128)(2,1)}), bf16[4,8,8192]{2,1,0:T(8,128)(2,1)S(1)}, u32[]{:S(2)}, u32[]{:S(2)}) async-start(bf16[4,8,8192]{2,1,0:T(8,128)(2,1)} %bitcast.83), calls=%async_computation.2 | async-start | bytes 1048576 | tf_op jit(solution)/shard_map/all_to_all | solution.py:35
  27.2 8.6 all-to-all-start.1
  35.8 330.3 %copy-start.2 = (f32[8192]{0:T(1024)S(1)}, f32[8192]{0:T(1024)}, u32[]{:S(2)}) copy-start(f32[8192]{0:T(1024)} %param.21) | copy-start | bytes 98308
  423.0 22.6 %copy-start.3 = (f32[4096]{0:T(1024)S(1)}, f32[4096]{0:T(1024)}, u32[]{:S(2)}) copy-start(f32[4096]{0:T(1024)} %param.23) | copy-start | bytes 49156
  427.5 8.6 all-to-all-start.3
  436.1 8.6 all-to-all-start.4
  446.8 8.6 all-to-all-start.5
  844.7 8.6 all-to-all-start.6
  853.3 8.6 all-to-all-start.7
  863.9 8.6 all-to-all-start.8
  1256.9 23.2 %copy-start.4 = (f32[16,4,128]{2,1,0:T(4,128)}, f32[16,4,128]{2,1,0:T(4,128)S(1)}, u32[]{:S(2)}) copy-start(f32[16,4,128]{2,1,0:T(4,128)S(1)} %get-tuple-element.1243) | copy-start | bytes 98308
  1261.5 8.6 all-to-all-start.9
  1270.1 8.6 all-to-all-start.10
where the time goes:
time: 1290 us; the launch traced here: 1280 us
  blocking collectives  746 us (58%)
  matrix products  202 us (16%)
  local copies, waits for them, and re-layouts  183 us (14%)
  other arithmetic  61.7 us (5%)
  waiting for transfers between devices  42 us (3%)
  starting transfers between devices  38.8 us (3%)
    pmax x3, blocking collectives, shards(): lax.pmax(row_top.astype(jnp.bfloat16), 'grp').astype(row_top.dtype)  374 us
    psum x3, blocking collectives, shards(): lax.psum((row_mass * jnp.exp(row_top - highest)).astype(jnp.bfloat16), 'g...  372 us
    dot_general x96, matrix products, tile_cost(): jnp.einsum('bid,bkjd->bkij', block_points, others, preferred_element_type...  202 us
    gather x96, local copies, waits for them, and re-layouts, tile_cost(): others = fetched[block_slots]  71.9 us
    gather x96, local copies, waits for them, and re-layouts, tile_cost(): target_sq[block_slots][:, :, None, :]  55.1 us
    gather x48, local copies, waits for them, and re-layouts, row_turn(): pot_table[block_slots][:, :, None, :]  27.5 us
  transfers between devices with their start and end apart: 11, of which 10 were waited for; matrix products, arithmetic and copies ran while one was open for 2% of the time, Pallas kernels for 0%

commit v1 on v0

v1 whole, which is shorter than its diff:
```python
import functools

import jax
import jax.numpy as jnp
from jax import lax
from jax.experimental import pallas as pl
from jax.experimental.pallas import tpu as pltpu
from jax.sharding import PartitionSpec as P

D = 64
BLOCK = 128
KG = 8
ITERS = 3
EPSILON = 0.25
LOWEST = -1e30
LOG2E = 1.4426950408889634
SCALE = LOG2E / EPSILON
UNROLL = 8
GROUP = 32


def plan_kernel(blocks, slots_ref, counts_ref, block_ref, slot_ref, total_ref):
    def one_block(b, position):
        for k in range(KG):
            block_ref[position + k] = b
            slot_ref[position + k] = slots_ref[b * KG + k]
        return position + counts_ref[b]

    total = lax.fori_loop(0, blocks, one_block, jnp.int32(0))
    for k in range(UNROLL):
        block_ref[total + k] = blocks
        slot_ref[total + k] = GROUP
    total_ref[0] = (total + UNROLL - 1) // UNROLL


def plan(tile_slot, tile_counts):
    blocks = tile_counts.shape[0]
    room = blocks * KG + UNROLL + KG
    smem = pl.BlockSpec(memory_space=pltpu.SMEM)
    return pl.pallas_call(
        functools.partial(plan_kernel, blocks),
        out_shape=(
            jax.ShapeDtypeStruct((room,), jnp.int32),
            jax.ShapeDtypeStruct((room,), jnp.int32),
            jax.ShapeDtypeStruct((1,), jnp.int32),
        ),
        in_specs=[smem, smem],
        out_specs=(smem, smem, smem),
    )(tile_slot.reshape(-1), tile_counts.reshape(-1))


def split3(values):
    high = values.astype(jnp.bfloat16)
    rest = values - high.astype(jnp.float32)
    middle = rest.astype(jnp.bfloat16)
    low = (rest - middle.astype(jnp.float32)).astype(jnp.bfloat16)
    return high, middle, low


def nt_dot(left, right):
    return lax.dot_general(left, right, (((1,), (1,)), ((), ())), preferred_element_type=jnp.float32)


def pass_kernel(
    total_ref, left_ids, right_ids, left_ref, right_ref, bias_ref, out_ref, columns, peaks, masses
):
    lefts, rights = left_ref.shape[0], right_ref.shape[0]
    diagonal = lax.broadcasted_iota(jnp.int32, (BLOCK, BLOCK), 0) == lax.broadcasted_iota(
        jnp.int32, (BLOCK, BLOCK), 1
    )
    eye = jnp.where(diagonal, 1.0, 0.0).astype(jnp.bfloat16)
    for group in range(lefts // GROUP):
        high, middle, low = split3(bias_ref[group * GROUP : (group + 1) * GROUP, :])
        parts = jnp.concatenate([high, middle, low, jnp.zeros_like(high)], axis=0)
        columns[group] = nt_dot(eye, parts).astype(jnp.bfloat16)
    peaks[...] = jnp.full_like(peaks, LOWEST)
    masses[...] = jnp.zeros_like(masses)
    lane = lax.broadcasted_iota(jnp.int32, (BLOCK, BLOCK), 1)
    lane = jnp.where(lane < 3 * GROUP, lane % GROUP, -1)

    def step(t, carry):
        for u in range(UNROLL):
            left_id = jnp.minimum(left_ids[t * UNROLL + u], lefts - 1)
            right_id = right_ids[t * UNROLL + u]
            picked = jnp.where(lane == left_id % GROUP, 1.0, 0.0).astype(jnp.bfloat16)
            left = jnp.concatenate([left_ref[left_id], columns[left_id // GROUP]], axis=1)
            right = jnp.concatenate([right_ref[jnp.minimum(right_id, rights - 1)], picked], axis=1)
            scores = nt_dot(left, right).reshape(BLOCK // 8, 8, BLOCK)
            old = peaks[u, right_id]
            top = jnp.maximum(old, jnp.max(scores, axis=0))
            mass = jnp.sum(jnp.exp2(scores - top[None]), axis=0)
            masses[u, right_id] = masses[u, right_id] * jnp.exp2(old - top) + mass
            peaks[u, right_id] = top
        return carry

    lax.fori_loop(0, total_ref[0], step, 0)

    def finish(r, carry):
        tops = [peaks[u, r] for u in range(UNROLL)]
        top = functools.reduce(jnp.maximum, tops)
        top = jnp.max(top, axis=0, keepdims=True)
        mass = sum(masses[u, r] * jnp.exp2(tops[u] - top) for u in range(UNROLL))
        mass = jnp.sum(mass, axis=0, keepdims=True)
        out_ref[pl.ds(r, 1), :] = top + jnp.log2(mass)
        return carry

    lax.fori_loop(0, rights, finish, 0, unroll=8)


def log_sums(total, left_ids, right_ids, left, right, bias):
    smem = pl.BlockSpec(memory_space=pltpu.SMEM)
    vmem = pl.BlockSpec(memory_space=pltpu.VMEM)
    rights = right.shape[0]
    return pl.pallas_call(
        pass_kernel,
        out_shape=jax.ShapeDtypeStruct((rights, BLOCK), jnp.float32),
        in_specs=[smem, smem, smem, vmem, vmem, vmem],
        out_specs=vmem,
        scratch_shapes=[
            pltpu.VMEM((left.shape[0] // GROUP, BLOCK, BLOCK), jnp.bfloat16),
            pltpu.VMEM((UNROLL, rights + 1, 8, BLOCK), jnp.float32),
            pltpu.VMEM((UNROLL, rights + 1, 8, BLOCK), jnp.float32),
        ],
        compiler_params=pltpu.CompilerParams(vmem_limit_bytes=40 * 1024 * 1024),
    )(total, left_ids, right_ids, left, right, bias)


def combine(values, axis):
    top = jnp.max(values, axis=axis, keepdims=True)
    return jnp.squeeze(top, axis) + jnp.log2(jnp.sum(jnp.exp2(values - top), axis=axis))


def shards(
    source_points,
    source_logmass,
    target_points,
    target_logmass,
    target_potential,
    tile_slot,
    tile_counts,
    fetch_ids,
):
    peers = lax.axis_size("src")
    groups = lax.axis_size("grp")
    blocks = tile_counts.shape[0]
    per_peer = fetch_ids.shape[1]
    owned = target_potential.shape[0] // BLOCK
    fetched_count = peers * per_peer
    sources = source_points.shape[0]
    share = sources // groups

    def across(values):
        return lax.all_to_all(values, "src", split_axis=0, concat_axis=0, tiled=True)

    block_list, slot_list, total = plan(tile_slot, tile_counts)
    requested = across(fetch_ids)
    target_sq = jnp.sum(jnp.square(target_points.astype(jnp.float32)), -1)
    start = SCALE * (target_potential - 0.5 * target_sq)
    halves = target_points.reshape(owned, 2, BLOCK // 2, D)
    packed = jnp.concatenate([halves[:, 0], halves[:, 1]], axis=-1)
    fetched = across(packed[requested]).reshape(fetched_count, BLOCK // 2, 2 * D)
    mass_rows = LOG2E * target_logmass.reshape(owned, BLOCK)
    potentials = across(start.reshape(owned, BLOCK)[requested]).reshape(fetched_count, BLOCK)
    low_half, high_half = fetched[:, :, :D], fetched[:, :, D:]
    targets = jnp.concatenate(
        [
            jnp.concatenate([low_half, low_half], axis=-1),
            jnp.concatenate([high_half, high_half], axis=-1),
        ],
        axis=1,
    )
    wide = source_points.astype(jnp.float32)
    source_sq = jnp.sum(jnp.square(wide), -1)
    scaled = SCALE * wide
    high = lax.reduce_precision(scaled, 8, 7)
    points = jnp.concatenate(
        [high.astype(jnp.bfloat16), (scaled - high).astype(jnp.bfloat16)], axis=-1
    ).reshape(blocks, BLOCK, 2 * D)
    my_mass = LOG2E * lax.dynamic_slice(
        source_logmass, (lax.axis_index("grp") * share,), (share,)
    )
    mine = jnp.arange(owned, dtype=jnp.int32)[:, None, None] == requested[None]

    for sweep_index in range(ITERS):
        rows = log_sums(total, slot_list, block_list, targets, points, potentials)
        rows = lax.all_to_all(rows.reshape(groups, share), "grp", 0, 0, tiled=True)
        field = my_mass - combine(rows, 0)
        field = lax.all_to_all(
            jnp.broadcast_to(field[None], (groups, share)), "grp", 0, 0, tiled=True
        ).reshape(blocks, BLOCK)
        cols = log_sums(total, block_list, slot_list, points, targets, field)
        back = across(cols.reshape(peers, per_peer, BLOCK))
        parts = jnp.max(jnp.where(mine[..., None], back[None], LOWEST), axis=2)
        owned_pot = mass_rows - combine(parts, 1)
        if sweep_index < ITERS - 1:
            potentials = across(owned_pot[requested]).reshape(fetched_count, BLOCK)
    source_field = field.reshape(-1) * (1.0 / SCALE) + 0.5 * source_sq
    target_field = owned_pot.reshape(-1) * (1.0 / SCALE) + 0.5 * target_sq
    return (source_field, target_field)


def solution(mesh):
    return jax.shard_map(
        shards,
        mesh=mesh,
        in_specs=(
            P("src", None),
            P("src"),
            P(("src", "grp"), None),
            P(("src", "grp")),
            P(("src", "grp")),
            P("src", "grp"),
            P("src", "grp"),
            P("src", "grp"),
        ),
        out_specs=(P("src"), P(("src", "grp"))),
        check_vma=False,
    )
```

time: 1290 us -> 274 us (0.21)
  the two profiles are of different devices: /device:TPU:0 before, /device:TPU:57 now
where the time goes in v1:
time: 274 us
  Pallas kernels  117 us (43%)
  blocking collectives  82 us (30%)
  starting transfers between devices  30.7 us (11%)
  local copies, waits for them, and re-layouts  17.3 us (6%)
  waiting for transfers between devices  15.7 us (6%)
  other arithmetic  10.1 us (4%)
    pallas_call x6, Pallas kernels, log_sums(): pl.pallas_call(pass_kernel, out_shape=jax.ShapeDtypeStruct((rights, BLOCK...  115 us
    all_to_all x3, blocking collectives, shards(): lax.all_to_all(jnp.broadcast_to(field[None], (groups, share)), 'grp', 0,...  32.2 us
    all_to_all x2, blocking collectives, shards(): rows = lax.all_to_all(rows.reshape(groups, share), 'grp', 0, 0, tiled=True)  30.1 us
    all_to_all x3, blocking collectives, across(): lax.all_to_all(values, 'src', split_axis=0, concat_axis=0, tiled=True)  19.7 us
    all_to_all x5, starting transfers between devices, across(): lax.all_to_all(values, 'src', split_axis=0, concat_axis=0, tiled=True)  19 us
    all_to_all x1, starting transfers between devices, shards(): rows = lax.all_to_all(rows.reshape(groups, share), 'grp', 0, 0, tiled=True)  11.7 us
    all_to_all x5, waiting for transfers between devices, across(): lax.all_to_all(values, 'src', split_axis=0, concat_axis=0, tiled=True)  11 us
  transfers between devices with their start and end apart: 6, of which 4 were waited for; matrix products, arithmetic and copies ran while one was open for 7% of the time, Pallas kernels for 1%

profile of v1, /device:TPU:57, one launch (start us, length us, event | category | flops | bytes accessed | tf_op | source)
XLA Modules:
  0.0 274.1 jit_solution(6436088165900917239)
XLA Ops:
  0.6 4.0 %all-to-all-start = ((s32[4,1,8]{2,1,0:T(1,128)}), s32[4,1,8]{2,1,0:T(1,128)S(1)}, u32[]{:S(2)}, u32[]{:S(2)}) async-start(s32[4,1,8]{2,1,0:T(1,128)} %bitcast.89), calls=%async_computation | async-start | bytes 4096 | tf_op jit(solution)/shard_map/all_to_all | solution.py:153
  4.7 2.7 reshape.141
  7.4 2.4 fusion.13
  9.8 2.0 copy.44
  11.8 0.9 copy.29
  12.7 1.8 fusion
  14.5 1.1 pad_maximum_fusion.1
  15.7 2.5 gather_fusion
  18.2 4.2 %all-to-all-start.1 = ((bf16[4,8,64,128]{3,2,1,0:T(8,128)(2,1)}), bf16[4,8,64,128]{3,2,1,0:T(8,128)(2,1)S(1)}, u32[]{:S(2)}, u32[]{:S(2)}) async-start(bf16[4,8,64,128]{3,2,1,0:T(8,128)(2,1)} %bitcast.6), calls=%async_computation.1 | async-start | bytes 1048576 | tf_op jit(solution)/shard_map/all_to_all | solution.py:153
  22.4 1.5 pad_maximum_fusion
  23.9 3.3 %copy.31 = bf16[8192,128]{1,0:T(8,128)(2,1)S(1)} copy(bf16[8192,128]{0,1:T(8,128)(2,1)} %pad_maximum_fusion) | data formatting | bytes 4194304 | tf_op jit(solution)/shard_map/concatenate | solution.py:176
  27.3 0.7 reshape.139.slots_ref
  28.0 2.5 shard_map.95
  30.7 1.2 gather_fusion.1
  31.8 4.2 %all-to-all-start.2 = ((f32[4,8,128]{2,1,0:T(8,128)}), f32[4,8,128]{2,1,0:T(8,128)S(1)}, u32[]{:S(2)}, u32[]{:S(2)}) async-start(f32[4,8,128]{2,1,0:T(8,128)} %bitcast.12), calls=%async_computation.2 | async-start | bytes 32768 | tf_op jit(solution)/shard_map/all_to_all | solution.py:153
  36.1 0.2 fusion.14
  36.3 0.6 maximum_maximum_fusion.left_ref.right_ref
  36.9 3.4 %all-to-all-done.2 = f32[4,8,128]{2,1,0:T(8,128)S(1)} async-done(((f32[4,8,128]{2,1,0:T(8,128)}), f32[4,8,128]{2,1,0:T(8,128)S(1)}, u32[]{:S(2)}, u32[]{:S(2)}) %all-to-all-start.2) | async-done | bytes 16416 | tf_op jit(solution)/shard_map/all_to_all | solution.py:153
  40.3 19.7 %shard_map.96 = f32[64,128]{1,0:T(8,128)} custom-call(s32[1]{0:T(128)} %get-tuple-element.5.total_ref, s32[528]{0:T(1024)S(1)} %copy-done.1, s32[528]{0:T(1024)S(1)} %copy-done, bf16[32,128,128]{2,1,0:T(8,128)(2,1)S(1)} %maximum_maximum_fusion.left_ref.right_ref, bf16[64,128,128]{2,1,0:T(8,128)(2,1)S(1)} %bitcast.66, f32[32,128]{1,0:T(8,128)S(1)} %bitcast.77), custom_call_target="tpu_custom_call" | custom-call | tf_op jit(solution)/shard_map/pallas_call | solution.py:114
  60.0 11.7 %all-to-all-start.3 = ((f32[32,1,256]{2,1,0:T(1,128)}), f32[32,1,256]{2,1,0:T(1,128)S(1)}, u32[]{:S(2)}, u32[]{:S(2)}) async-start(f32[32,1,256]{2,1,0:T(1,128)} %bitcast.14), calls=%async_computation.3 | async-start | bytes 65536 | tf_op jit(solution)/shard_map/all_to_all | solution.py:186
  71.7 4.7 %all-to-all-done.3 = f32[32,1,256]{2,1,0:T(1,128)S(1)} async-done(((f32[32,1,256]{2,1,0:T(1,128)}), f32[32,1,256]{2,1,0:T(1,128)S(1)}, u32[]{:S(2)}, u32[]{:S(2)}) %all-to-all-start.3) | async-done | bytes 32800 | tf_op jit(solution)/shard_map/all_to_all | solution.py:186
  76.5 0.8 add_subtract_fusion.2
  77.3 10.7 %all_to_all.101 = f32[32,1,256]{2,1,0:T(1,128)S(1)} all-to-all(f32[32,1,256]{2,1,0:T(1,128)S(1)} %broadcast_in_dim.75), channel_id=1, replica_groups=mesh['src'=4,'grp'=32] {'grp'}, dimensions={0} | all-to-all | bytes 65536 | tf_op jit(solution)/shard_map/all_to_all | solution.py:188
  88.1 19.2 %shard_map.97 = f32[32,128]{1,0:T(8,128)} custom-call(s32[1]{0:T(128)} %get-tuple-element.5.total_ref, s32[528]{0:T(1024)S(1)} %copy-done, s32[528]{0:T(1024)S(1)} %copy-done.1, bf16[64,128,128]{2,1,0:T(8,128)(2,1)S(1)} %bitcast.67, bf16[32,128,128]{2,1,0:T(8,128)(2,1)S(1)} %maximum_maximum_fusion.left_ref.right_ref, f32[64,128]{1,0:T(8,128)S(1)} %bitcast.73), custom_call_target="tpu_custom_call" | custom-call | tf_op jit(solution)/shard_map/pallas_call | solution.py:114
  107.3 3.3 %all-to-all-start.5 = ((f32[4,8,128]{2,1,0:T(8,128)}), f32[4,8,128]{2,1,0:T(8,128)S(1)}, u32[]{:S(2)}, u32[]{:S(2)}) async-start(f32[4,8,128]{2,1,0:T(8,128)} %bitcast.16), calls=%async_computation.5 | async-start | bytes 32768 | tf_op jit(solution)/shard_map/all_to_all | solution.py:153
  110.6 4.1 %all-to-all-done.5 = f32[4,8,128]{2,1,0:T(8,128)S(1)} async-done(((f32[4,8,128]{2,1,0:T(8,128)}), f32[4,8,128]{2,1,0:T(8,128)S(1)}, u32[]{:S(2)}, u32[]{:S(2)}) %all-to-all-start.5) | async-done | bytes 16416 | tf_op jit(solution)/shard_map/all_to_all | solution.py:153
  114.7 0.3 select_reduce_fusion.4
  115.1 0.6 gather_fusion.2
  115.7 6.6 %all_to_all.102 = f32[4,8,128]{2,1,0:T(8,128)S(1)} all-to-all(f32[4,8,128]{2,1,0:T(8,128)S(1)} %bitcast.86), channel_id=1, replica_groups=mesh['src'=4,'grp'=32] {'src'}, dimensions={0} | all-to-all | bytes 32768 | tf_op jit(solution)/shard_map/all_to_all | solution.py:153
  122.3 19.1 %shard_map.98 = f32[64,128]{1,0:T(8,128)S(1)} custom-call(s32[1]{0:T(128)} %get-tuple-element.5.total_ref, s32[528]{0:T(1024)S(1)} %copy-done.1, s32[528]{0:T(1024)S(1)} %copy-done, bf16[32,128,128]{2,1,0:T(8,128)(2,1)S(1)} %maximum_maximum_fusion.left_ref.right_ref, bf16[64,128,128]{2,1,0:T(8,128)(2,1)S(1)} %bitcast.68, f32[32,128]{1,0:T(8,128)S(1)} %bitcast.78), custom_call_target="tpu_custom_call" | custom-call | tf_op jit(solution)/shard_map/pallas_call | solution.py:114
  141.3 15.0 %all_to_all.103 = f32[32,1,256]{2,1,0:T(1,128)S(1)} all-to-all(f32[32,1,256]{2,1,0:T(1,128)S(1)} %bitcast.74), channel_id=1, replica_groups=mesh['src'=4,'grp'=32] {'grp'}, dimensions={0} | all-to-all | bytes 65536 | tf_op jit(solution)/shard_map/all_to_all | solution.py:186
  156.5 0.8 add_subtract_fusion.1
  157.2 10.7 %all_to_all.104 = f32[32,1,256]{2,1,0:T(1,128)S(1)} all-to-all(f32[32,1,256]{2,1,0:T(1,128)S(1)} %broadcast_in_dim.78), channel_id=1, replica_groups=mesh['src'=4,'grp'=32] {'grp'}, dimensions={0} | all-to-all | bytes 65536 | tf_op jit(solution)/shard_map/all_to_all | solution.py:188
  168.0 18.6 %shard_map.99 = f32[32,128]{1,0:T(8,128)S(1)} custom-call(s32[1]{0:T(128)} %get-tuple-element.5.total_ref, s32[528]{0:T(1024)S(1)} %copy-done, s32[528]{0:T(1024)S(1)} %copy-done.1, bf16[64,128,128]{2,1,0:T(8,128)(2,1)S(1)} %bitcast.69, bf16[32,128,128]{2,1,0:T(8,128)(2,1)S(1)} %maximum_maximum_fusion.left_ref.right_ref, f32[64,128]{1,0:T(8,128)S(1)} %bitcast.75), custom_call_target="tpu_custom_call" | custom-call | tf_op jit(solution)/shard_map/pallas_call | solution.py:114
  186.6 6.6 %all_to_all.105 = f32[4,8,128]{2,1,0:T(8,128)S(1)} all-to-all(f32[4,8,128]{2,1,0:T(8,128)S(1)} %bitcast.79), channel_id=1, replica_groups=mesh['src'=4,'grp'=32] {'src'}, dimensions={0} | all-to-all | bytes 32768 | tf_op jit(solution)/shard_map/all_to_all | solution.py:153
  193.2 0.3 select_reduce_fusion.2
  193.6 0.6 gather_fusion.3
  194.1 6.6 %all_to_all.106 = f32[4,8,128]{2,1,0:T(8,128)S(1)} all-to-all(f32[4,8,128]{2,1,0:T(8,128)S(1)} %bitcast.85), channel_id=1, replica_groups=mesh['src'=4,'grp'=32] {'src'}, dimensions={0} | all-to-all | bytes 32768 | tf_op jit(solution)/shard_map/all_to_all | solution.py:153
  200.7 19.1 %shard_map.100 = f32[64,128]{1,0:T(8,128)S(1)} custom-call(s32[1]{0:T(128)} %get-tuple-element.5.total_ref, s32[528]{0:T(1024)S(1)} %copy-done.1, s32[528]{0:T(1024)S(1)} %copy-done, bf16[32,128,128]{2,1,0:T(8,128)(2,1)S(1)} %maximum_maximum_fusion.left_ref.right_ref, bf16[64,128,128]{2,1,0:T(8,128)(2,1)S(1)} %bitcast.70, f32[32,128]{1,0:T(8,128)S(1)} %bitcast.80), custom_call_target="tpu_custom_call" | custom-call | tf_op jit(solution)/shard_map/pallas_call | solution.py:114
  219.8 15.0 %all_to_all.107 = f32[32,1,256]{2,1,0:T(1,128)S(1)} all-to-all(f32[32,1,256]{2,1,0:T(1,128)S(1)} %bitcast.76), channel_id=1, replica_groups=mesh['src'=4,'grp'=32] {'grp'}, dimensions={0} | all-to-all | bytes 65536 | tf_op jit(solution)/shard_map/all_to_all | solution.py:186
  234.9 0.8 add_subtract_fusion
  235.7 10.7 %all_to_all.108 = f32[32,1,256]{2,1,0:T(1,128)S(1)} all-to-all(f32[32,1,256]{2,1,0:T(1,128)S(1)} %broadcast_in_dim.80), channel_id=1, replica_groups=mesh['src'=4,'grp'=32] {'grp'}, dimensions={0} | all-to-all | bytes 65536 | tf_op jit(solution)/shard_map/all_to_all | solution.py:188
  246.4 19.2 %shard_map.101 = f32[32,128]{1,0:T(8,128)} custom-call(s32[1]{0:T(128)} %get-tuple-element.5.total_ref, s32[528]{0:T(1024)S(1)} %copy-done, s32[528]{0:T(1024)S(1)} %copy-done.1, bf16[64,128,128]{2,1,0:T(8,128)(2,1)S(1)} %bitcast.71, bf16[32,128,128]{2,1,0:T(8,128)(2,1)S(1)} %maximum_maximum_fusion.left_ref.right_ref, f32[64,128]{1,0:T(8,128)S(1)} %bitcast.72), custom_call_target="tpu_custom_call" | custom-call | tf_op jit(solution)/shard_map/pallas_call | solution.py:114
  265.7 3.3 %all-to-all-start.13 = ((f32[4,8,128]{2,1,0:T(8,128)}), f32[4,8,128]{2,1,0:T(8,128)S(1)}, u32[]{:S(2)}, u32[]{:S(2)}) async-start(f32[4,8,128]{2,1,0:T(8,128)} %bitcast.27), calls=%async_computation.13 | async-start | bytes 32768 | tf_op jit(solution)/shard_map/all_to_all | solution.py:153
  269.0 0.6 multiply_add_fusion
  269.6 3.5 %all-to-all-done.13 = f32[4,8,128]{2,1,0:T(8,128)S(1)} async-done(((f32[4,8,128]{2,1,0:T(8,128)}), f32[4,8,128]{2,1,0:T(8,128)S(1)}, u32[]{:S(2)}, u32[]{:S(2)}) %all-to-all-start.13) | async-done | bytes 16416 | tf_op jit(solution)/shard_map/all_to_all | solution.py:153
  273.1 0.3 select_reduce_fusion
  273.5 0.6 fusion.12
  (38 shorter events, 0.9 us)
Async XLA Ops:
  0.6 15.0 %all-to-all-start = ((s32[4,1,8]{2,1,0:T(1,128)}), s32[4,1,8]{2,1,0:T(1,128)S(1)}, u32[]{:S(2)}, u32[]{:S(2)}) async-start(s32[4,1,8]{2,1,0:T(1,128)} %bitcast.89), calls=%async_computation | async-start | bytes 4096 | tf_op jit(solution)/shard_map/all_to_all | solution.py:153
  11.8 2.7 copy-start.2
  18.2 13.6 %all-to-all-start.1 = ((bf16[4,8,64,128]{3,2,1,0:T(8,128)(2,1)}), bf16[4,8,64,128]{3,2,1,0:T(8,128)(2,1)S(1)}, u32[]{:S(2)}, u32[]{:S(2)}) async-start(bf16[4,8,64,128]{3,2,1,0:T(8,128)(2,1)} %bitcast.6), calls=%async_computation.1 | async-start | bytes 1048576 | tf_op jit(solution)/shard_map/all_to_all | solution.py:153
  23.9 3.3 %copy-start.6 = (s32[64,8]{0,1:T(8,128)S(1)}, s32[64,8]{0,1:T(8,128)}, u32[]{:S(2)}) copy-start(s32[64,8]{0,1:T(8,128)} %param.13) | copy-start | bytes 6148
  23.9 6.6 %copy-start.3 = (bf16[4096,64]{0,1:T(8,128)(2,1)S(1)}, bf16[4096,64]{0,1:T(8,128)(2,1)}, u32[]{:S(2)}) copy-start(bf16[4096,64]{0,1:T(8,128)(2,1)} %param.10) | copy-start | bytes 1572868
  23.9 6.7 %copy-start.5 = (f32[4096]{0:T(1024)S(1)}, f32[4096]{0:T(1024)}, u32[]{:S(2)}) copy-start(f32[4096]{0:T(1024)} %param.12) | copy-start | bytes 49156
  31.8 8.5 %all-to-all-start.2 = ((f32[4,8,128]{2,1,0:T(8,128)}), f32[4,8,128]{2,1,0:T(8,128)S(1)}, u32[]{:S(2)}, u32[]{:S(2)}) async-start(f32[4,8,128]{2,1,0:T(8,128)} %bitcast.12), calls=%async_computation.2 | async-start | bytes 32768 | tf_op jit(solution)/shard_map/all_to_all | solution.py:153
  36.1 4.2 %copy-start = (s32[528]{0:T(1024)S(1)}, s32[528]{0:T(1024)}, u32[]{:S(2)}) copy-start(s32[528]{0:T(1024)} %get-tuple-element.7.right_ids.left_ids) | copy-start | bytes 6340
  36.1 4.2 %copy-start.1 = (s32[528]{0:T(1024)S(1)}, s32[528]{0:T(1024)}, u32[]{:S(2)}) copy-start(s32[528]{0:T(1024)} %get-tuple-element.6.left_ids.right_ids) | copy-start | bytes 6340
  60.0 55.1 %copy-start.4 = (f32[4096]{0:T(1024)S(1)}, f32[4096]{0:T(1024)}, u32[]{:S(2)}) copy-start(f32[4096]{0:T(1024)} %param.11) | copy-start | bytes 49156
  60.0 16.4 %all-to-all-start.3 = ((f32[32,1,256]{2,1,0:T(1,128)}), f32[32,1,256]{2,1,0:T(1,128)S(1)}, u32[]{:S(2)}, u32[]{:S(2)}) async-start(f32[32,1,256]{2,1,0:T(1,128)} %bitcast.14), calls=%async_computation.3 | async-start | bytes 65536 | tf_op jit(solution)/shard_map/all_to_all | solution.py:186
  107.3 7.4 %all-to-all-start.5 = ((f32[4,8,128]{2,1,0:T(8,128)}), f32[4,8,128]{2,1,0:T(8,128)S(1)}, u32[]{:S(2)}, u32[]{:S(2)}) async-start(f32[4,8,128]{2,1,0:T(8,128)} %bitcast.16), calls=%async_computation.5 | async-start | bytes 32768 | tf_op jit(solution)/shard_map/all_to_all | solution.py:153
  265.7 7.4 %all-to-all-start.13 = ((f32[4,8,128]{2,1,0:T(8,128)}), f32[4,8,128]{2,1,0:T(8,128)S(1)}, u32[]{:S(2)}, u32[]{:S(2)}) async-start(f32[4,8,128]{2,1,0:T(8,128)} %bitcast.27), calls=%async_computation.13 | async-start | bytes 32768 | tf_op jit(solution)/shard_map/all_to_all | solution.py:153

commit v2 on v1

v2 whole, which is shorter than its diff:
```python
import functools

import jax
import jax.numpy as jnp
from jax import lax
from jax.experimental import pallas as pl
from jax.experimental.pallas import tpu as pltpu
from jax.sharding import PartitionSpec as P

D = 64
BLOCK = 128
KG = 8
ITERS = 3
EPSILON = 0.25
LOWEST = -1e30
LOG2E = 1.4426950408889634
SCALE = LOG2E / EPSILON
PAIRS = 32
COPIES = 2
GROUP = 32


def plan_kernel(
    blocks, slots_ref, counts_ref, col_left, col_right, col_total, row_left, row_right, row_total, lists, sizes
):
    stride = blocks + KG
    for q in range(GROUP + 1):
        sizes[q] = 0

    def one_block(b, position):
        count = counts_ref[b]
        for k in range(KG):
            live = k < count
            slot = jnp.where(live, slots_ref[b * KG + k], GROUP)
            if k % 2 == 0:
                col_left[position + k // 2] = b
            col_right[2 * position + k] = slot
            size = sizes[slot]
            lists[slot * stride + size] = b
            sizes[slot] = jnp.where(live, size + 1, 0)
        return position + (count + 1) // 2

    total = lax.fori_loop(0, blocks, one_block, jnp.int32(0))
    col_total[0] = (total + PAIRS - 1) // PAIRS

    def pad_cols(k, carry):
        col_left[total + k] = 0
        col_right[2 * (total + k)] = GROUP
        col_right[2 * (total + k) + 1] = GROUP
        return carry

    lax.fori_loop(0, PAIRS, pad_cols, 0)

    def one_slot(q, position):
        size = sizes[q]
        lists[q * stride + size] = blocks

        def one_pair(k, carry):
            row_left[position + k] = q
            row_right[2 * (position + k)] = lists[q * stride + 2 * k]
            row_right[2 * (position + k) + 1] = lists[q * stride + 2 * k + 1]
            return carry

        lax.fori_loop(0, (size + 1) // 2, one_pair, 0)
        return position + (size + 1) // 2

    rows = lax.fori_loop(0, GROUP, one_slot, jnp.int32(0))
    row_total[0] = (rows + PAIRS - 1) // PAIRS

    def pad_rows(k, carry):
        row_left[rows + k] = 0
        row_right[2 * (rows + k)] = blocks
        row_right[2 * (rows + k) + 1] = blocks
        return carry

    lax.fori_loop(0, PAIRS, pad_rows, 0)


def plan(tile_slot, tile_counts):
    blocks = tile_counts.shape[0]
    col_room = blocks * KG // 2 + PAIRS + KG
    row_room = blocks * KG // 2 + GROUP + PAIRS
    smem = pl.BlockSpec(memory_space=pltpu.SMEM)
    shapes = [(col_room,), (2 * col_room,), (1,), (row_room,), (2 * row_room,), (1,)]
    out = pl.pallas_call(
        functools.partial(plan_kernel, blocks),
        out_shape=[jax.ShapeDtypeStruct(shape, jnp.int32) for shape in shapes],
        in_specs=[smem, smem],
        out_specs=[smem] * len(shapes),
        scratch_shapes=[
            pltpu.SMEM(((GROUP + 1) * (blocks + KG),), jnp.int32),
            pltpu.SMEM((GROUP + 1,), jnp.int32),
        ],
    )(tile_slot.reshape(-1), tile_counts.reshape(-1))
    return out[:3], out[3:]


def split3(values):
    high = values.astype(jnp.bfloat16)
    rest = values - high.astype(jnp.float32)
    middle = rest.astype(jnp.bfloat16)
    low = (rest - middle.astype(jnp.float32)).astype(jnp.bfloat16)
    return high, middle, low


def pass_kernel(
    left_ids, right_ids, total_ref, left_ref, right_ref, bias_ref, out_ref, columns, peaks, masses
):
    lefts, rights = left_ref.shape[0], right_ref.shape[0]
    square = (BLOCK, BLOCK)
    lane = lax.broadcasted_iota(jnp.int32, square, 1)
    eye = jnp.where(lane == lax.broadcasted_iota(jnp.int32, square, 0), 1.0, 0.0).astype(jnp.bfloat16)
    lane = jnp.where(lane < 3 * GROUP, lane % GROUP, -1)
    for group in range(lefts // GROUP):
        high, middle, low = split3(bias_ref[group * GROUP : (group + 1) * GROUP, :])
        parts = jnp.concatenate([high, middle, low, jnp.zeros_like(high)], axis=0)
        turned = lax.dot_general(
            eye, parts, (((1,), (1,)), ((), ())), preferred_element_type=jnp.float32
        )

        def fill(k, carry, group=group, turned=turned):
            columns[group * GROUP + k] = jnp.where(lane == k, turned, 0.0).astype(jnp.bfloat16)
            return carry

        lax.fori_loop(0, GROUP, fill, 0, unroll=4)
    peaks[...] = jnp.full_like(peaks, LOWEST)
    masses[...] = jnp.zeros_like(masses)
    ones = jnp.ones((BLOCK, 2 * BLOCK), jnp.bfloat16)

    def fold(copy, r, scores):
        scores = scores.reshape(BLOCK // 8, 8, BLOCK)
        old = peaks[copy, r]
        top = jnp.maximum(old, jnp.max(scores, axis=0))
        mass = jnp.sum(jnp.exp2(scores - top[None]), axis=0)
        masses[copy, r] = masses[copy, r] * jnp.exp2(old - top) + mass
        peaks[copy, r] = top

    def step(t, carry):
        for u in range(PAIRS):
            i = t * PAIRS + u
            l, first, second = left_ids[i], right_ids[2 * i], right_ids[2 * i + 1]
            left = jnp.concatenate([left_ref[l], columns[l]], axis=1)
            right = jnp.concatenate(
                [right_ref[jnp.minimum(first, rights - 1)], right_ref[jnp.minimum(second, rights - 1)]],
                axis=1,
            )
            scores = jnp.dot(
                left, jnp.concatenate([right, ones], axis=0), preferred_element_type=jnp.float32
            )
            fold((2 * u) % COPIES, first, scores[:, :BLOCK])
            fold((2 * u + 1) % COPIES, second, scores[:, BLOCK:])
        return carry

    lax.fori_loop(0, total_ref[0], step, 0)

    def finish(octet, carry):
        rows = []
        for k in range(8):
            r = octet * 8 + k
            tops = [peaks[copy, r] for copy in range(COPIES)]
            top = jnp.max(functools.reduce(jnp.maximum, tops), axis=0, keepdims=True)
            mass = sum(masses[copy, r] * jnp.exp2(tops[copy] - top) for copy in range(COPIES))
            rows.append(top + jnp.log2(jnp.sum(mass, axis=0, keepdims=True)))
        out_ref[pl.ds(pl.multiple_of(octet * 8, 8), 8), :] = jnp.concatenate(rows, axis=0)
        return carry

    lax.fori_loop(0, rights // 8, finish, 0)


def log_sums(pairs, left, right, bias):
    smem = pl.BlockSpec(memory_space=pltpu.SMEM)
    vmem = pl.BlockSpec(memory_space=pltpu.VMEM)
    lefts, rights = left.shape[0], right.shape[0]
    return pl.pallas_call(
        pass_kernel,
        out_shape=jax.ShapeDtypeStruct((rights, BLOCK), jnp.float32),
        in_specs=[smem, smem, smem, vmem, vmem, vmem],
        out_specs=vmem,
        scratch_shapes=[
            pltpu.VMEM((lefts, BLOCK, BLOCK), jnp.bfloat16),
            pltpu.VMEM((COPIES, rights + 1, 8, BLOCK), jnp.float32),
            pltpu.VMEM((COPIES, rights + 1, 8, BLOCK), jnp.float32),
        ],
        compiler_params=pltpu.CompilerParams(vmem_limit_bytes=40 * 1024 * 1024),
    )(*pairs, left, right, bias)


def combine(values, axis):
    top = jnp.max(values, axis=axis, keepdims=True)
    return jnp.squeeze(top, axis) + jnp.log2(jnp.sum(jnp.exp2(values - top), axis=axis))


def shards(
    source_points,
    source_logmass,
    target_points,
    target_logmass,
    target_potential,
    tile_slot,
    tile_counts,
    fetch_ids,
):
    peers = lax.axis_size("src")
    groups = lax.axis_size("grp")
    blocks = tile_counts.shape[0]
    per_peer = fetch_ids.shape[1]
    owned = target_potential.shape[0] // BLOCK
    fetched_count = peers * per_peer
    sources = source_points.shape[0]
    share = sources // groups

    def across(values):
        return lax.all_to_all(values, "src", split_axis=0, concat_axis=0, tiled=True)

    col_pairs, row_pairs = plan(tile_slot, tile_counts)
    requested = across(fetch_ids)
    target_sq = jnp.sum(jnp.square(target_points.astype(jnp.float32)), -1)
    start = SCALE * (target_potential - 0.5 * target_sq)
    halves = target_points.reshape(owned, 2, BLOCK // 2, D)
    packed = jnp.concatenate([halves[:, 0], halves[:, 1]], axis=-1)
    fetched = across(packed[requested]).reshape(fetched_count, BLOCK // 2, 2 * D)
    mass_rows = LOG2E * target_logmass.reshape(owned, BLOCK)
    potentials = across(start.reshape(owned, BLOCK)[requested]).reshape(fetched_count, BLOCK)
    low_half, high_half = fetched[:, :, :D], fetched[:, :, D:]
    targets = jnp.concatenate(
        [
            jnp.concatenate([low_half, low_half], axis=-1),
            jnp.concatenate([high_half, high_half], axis=-1),
        ],
        axis=1,
    )
    wide = source_points.astype(jnp.float32)
    source_sq = jnp.sum(jnp.square(wide), -1)
    scaled = SCALE * wide
    high = lax.reduce_precision(scaled, 8, 7)
    points = jnp.concatenate(
        [high.astype(jnp.bfloat16), (scaled - high).astype(jnp.bfloat16)], axis=-1
    ).reshape(blocks, BLOCK, 2 * D)
    points_turned = points.transpose(0, 2, 1)
    targets_turned = targets.transpose(0, 2, 1)
    my_mass = LOG2E * lax.dynamic_slice(
        source_logmass, (lax.axis_index("grp") * share,), (share,)
    )
    mine = jnp.arange(owned, dtype=jnp.int32)[:, None, None] == requested[None]

    for sweep_index in range(ITERS):
        rows = log_sums(row_pairs, targets, points_turned, potentials)
        rows = lax.all_to_all(rows.reshape(groups, share), "grp", 0, 0, tiled=True)
        field = my_mass - combine(rows, 0)
        field = lax.all_to_all(
            jnp.broadcast_to(field[None], (groups, share)), "grp", 0, 0, tiled=True
        ).reshape(blocks, BLOCK)
        cols = log_sums(col_pairs, points, targets_turned, field)
        back = across(cols.reshape(peers, per_peer, BLOCK))
        parts = jnp.max(jnp.where(mine[..., None], back[None], LOWEST), axis=2)
        owned_pot = mass_rows - combine(parts, 1)
        if sweep_index < ITERS - 1:
            potentials = across(owned_pot[requested]).reshape(fetched_count, BLOCK)
    source_field = field.reshape(-1) * (1.0 / SCALE) + 0.5 * source_sq
    target_field = owned_pot.reshape(-1) * (1.0 / SCALE) + 0.5 * target_sq
    return (source_field, target_field)


def solution(mesh):
    return jax.shard_map(
        shards,
        mesh=mesh,
        in_specs=(
            P("src", None),
            P("src"),
            P(("src", "grp"), None),
            P(("src", "grp")),
            P(("src", "grp")),
            P("src", "grp"),
            P("src", "grp"),
            P("src", "grp"),
        ),
        out_specs=(P("src"), P(("src", "grp"))),
        check_vma=False,
    )
```

time: 274 us -> 227 us (0.83)
  the two profiles are of different devices: /device:TPU:57 before, /device:TPU:0 now
where the time goes in v2:
time: 227 us; the launch traced here: 226 us
  blocking collectives  85.7 us (38%)
  starting transfers between devices  46.6 us (21%)
  local copies, waits for them, and re-layouts  33 us (15%)
  Pallas kernels  30.6 us (13%)
  waiting for transfers between devices  17.5 us (8%)
  other arithmetic  11.2 us (5%)
    all_to_all x5, starting transfers between devices, across(): lax.all_to_all(values, 'src', split_axis=0, concat_axis=0, tiled=True)  36.2 us
    all_to_all x3, blocking collectives, shards(): lax.all_to_all(jnp.broadcast_to(field[None], (groups, share)), 'grp', 0,...  32.2 us
    all_to_all x3, blocking collectives, across(): lax.all_to_all(values, 'src', split_axis=0, concat_axis=0, tiled=True)  31.8 us
    pallas_call x6, Pallas kernels, log_sums(): pl.pallas_call(pass_kernel, out_shape=jax.ShapeDtypeStruct((rights, BLOCK...  24.3 us
    all_to_all x2, blocking collectives, shards(): rows = lax.all_to_all(rows.reshape(groups, share), 'grp', 0, 0, tiled=True)  21.7 us
    unnamed x34, local copies, waits for them, and re-layouts  11.3 us
    all_to_all x1, starting transfers between devices, shards(): rows = lax.all_to_all(rows.reshape(groups, share), 'grp', 0, 0, tiled=True)  10.5 us
    all_to_all x5, waiting for transfers between devices, across(): lax.all_to_all(values, 'src', split_axis=0, concat_axis=0, tiled=True)  10 us
  transfers between devices with their start and end apart: 6, of which 3 were waited for; matrix products, arithmetic and copies ran while one was open for 12% of the time, Pallas kernels for 3%

profile of v2, /device:TPU:0, one launch (start us, length us, event | category | flops | bytes accessed | tf_op | source)
XLA Modules:
  0.0 225.6 jit_solution(9906143836747223136)
XLA Ops:
  0.6 4.4 %all-to-all-start = ((s32[4,1,8]{2,1,0:T(1,128)}), s32[4,1,8]{2,1,0:T(1,128)S(1)}, u32[]{:S(2)}, u32[]{:S(2)}) async-start(s32[4,1,8]{2,1,0:T(1,128)} %bitcast.91), calls=%async_computation | async-start | bytes 4096 | tf_op jit(solution)/shard_map/all_to_all | solution.py:213
  5.0 2.7 %reshape.141 = bf16[32,2,64,64]{2,1,0,3:T(2,128)(2,1)S(1)} reshape(bf16[4096,64]{0,1:T(8,128)(2,1)} %param.10) | data formatting | bytes 1048576 | tf_op jit(solution)/shard_map/reshape | solution.py:219
  7.8 2.4 %fusion.15 = (bf16[32,1,64,64]{2,1,0,3:T(2,128)(2,1)S(1)}, bf16[32,1,64,64]{2,1,0,3:T(2,128)(2,1)S(1)}) fusion(bf16[32,2,64,64]{2,1,0,3:T(2,128)(2,1)S(1)} %reshape.141), kind=kLoop, calls=%fused_computation.52 | loop fusion | bytes 1048576 | tf_op jit(solution)/shard_map/slice | solution.py:220
  10.2 2.0 copy.78
  12.2 0.9 copy.56
  13.1 1.8 fusion
  14.9 1.1 pad_maximum_fusion.1
  16.1 2.5 %gather_fusion = bf16[32,64,128]{2,1,0:T(8,128)(2,1)} fusion(bf16[32,64,128]{2,1,0:T(8,128)(2,1)} %pad_maximum_fusion.1, s32[1024]{0:T(1024)S(1)} %pad_clamp_fusion), kind=kCustom, calls=%fused_computation | custom fusion | bytes 1048704 | tf_op jit(solution)/shard_map/gather | solution.py:221
  18.5 4.8 %all-to-all-start.1 = ((bf16[4,8,64,128]{3,2,1,0:T(8,128)(2,1)}), bf16[4,8,64,128]{3,2,1,0:T(8,128)(2,1)S(1)}, u32[]{:S(2)}, u32[]{:S(2)}) async-start(bf16[4,8,64,128]{3,2,1,0:T(8,128)(2,1)} %bitcast.6), calls=%async_computation.1 | async-start | bytes 1048576 | tf_op jit(solution)/shard_map/all_to_all | solution.py:213
  23.3 1.5 pad_maximum_fusion
  25.6 3.2 %copy.59 = bf16[8192,128]{1,0:T(8,128)(2,1)S(1)} copy(bf16[8192,128]{0,1:T(8,128)(2,1)} %pad_maximum_fusion) | data formatting | bytes 4194304 | tf_op jit(solution)/shard_map/concatenate | solution.py:236
  28.9 2.9 %copy.69.right_ref = bf16[64,128,128]{2,1,0:T(8,128)(2,1)} copy(bf16[64,128,128]{1,2,0:T(8,128)(2,1)S(1)} %bitcast.70) | data formatting | bytes 4194304 | tf_op jit(solution)/shard_map/transpose | solution.py:239
  31.8 6.3 %shard_map.95 = (s32[296]{0:T(512)}, s32[592]{0:T(1024)}, s32[1]{0:T(128)}, s32[320]{0:T(512)}, s32[640]{0:T(1024)}, /*index=5*/s32[1]{0:T(128)}) custom-call(s32[512]{0:T(512)} %reshape.139.slots_ref, s32[64]{0:T(128)} %bitcast.92), custom_call_target="tpu_custom_call" | custom-call | tf_op jit(solution)/shard_map/pallas_call | solution.py:85
  38.3 1.2 gather_fusion.1
  39.5 0.8 copy-done.12
  40.3 5.5 %all-to-all-start.2 = ((f32[4,8,128]{2,1,0:T(8,128)}), f32[4,8,128]{2,1,0:T(8,128)S(1)}, u32[]{:S(2)}, u32[]{:S(2)}) async-start(f32[4,8,128]{2,1,0:T(8,128)} %bitcast.14), calls=%async_computation.2 | async-start | bytes 32768 | tf_op jit(solution)/shard_map/all_to_all | solution.py:213
  45.8 1.5 copy.58
  47.4 1.7 fusion.13
  49.1 2.3 %copy.68.left_ref = bf16[32,128,128]{2,1,0:T(8,128)(2,1)} copy(bf16[32,128,128]{1,2,0:T(8,128)(2,1)} %get-tuple-element.24) | data formatting | bytes 2097152 | tf_op jit(solution)/shard_map/concatenate | solution.py:225
  51.4 1.6 copy-done
  53.0 1.2 copy-done.3
  54.2 4.3 %shard_map.96 = f32[64,128]{1,0:T(8,128)} custom-call(s32[320]{0:T(512)S(1)} %copy-done.9, s32[640]{0:T(1024)S(1)} %copy-done.7, s32[1]{0:T(128)} %get-tuple-element.10.total_ref, bf16[32,128,128]{2,1,0:T(8,128)(2,1)S(1)} %copy-done.3, bf16[64,128,128]{2,1,0:T(8,128)(2,1)S(1)} %copy-done, f32[32,128]{1,0:T(8,128)S(1)} %bitcast.79), custom_call_target="tpu_custom_call" | custom-call | tf_op jit(solution)/shard_map/pallas_call | solution.py:174
  58.6 10.5 %all-to-all-start.3 = ((f32[32,1,256]{2,1,0:T(1,128)}), f32[32,1,256]{2,1,0:T(1,128)S(1)}, u32[]{:S(2)}, u32[]{:S(2)}) async-start(f32[32,1,256]{2,1,0:T(1,128)} %bitcast.16), calls=%async_computation.3 | async-start | bytes 65536 | tf_op jit(solution)/shard_map/all_to_all | solution.py:248
  69.0 7.4 %all-to-all-done.3 = f32[32,1,256]{2,1,0:T(1,128)S(1)} async-done(((f32[32,1,256]{2,1,0:T(1,128)}), f32[32,1,256]{2,1,0:T(1,128)S(1)}, u32[]{:S(2)}, u32[]{:S(2)}) %all-to-all-start.3) | async-done | bytes 32800 | tf_op jit(solution)/shard_map/all_to_all | solution.py:248
  76.5 0.8 add_subtract_fusion.2
  77.3 10.7 %all_to_all.101 = f32[32,1,256]{2,1,0:T(1,128)S(1)} all-to-all(f32[32,1,256]{2,1,0:T(1,128)S(1)} %broadcast_in_dim.75), channel_id=1, replica_groups=mesh['src'=4,'grp'=32] {'grp'}, dimensions={0} | all-to-all | bytes 65536 | tf_op jit(solution)/shard_map/all_to_all | solution.py:250
  88.1 4.4 %shard_map.97 = f32[32,128]{1,0:T(8,128)} custom-call(s32[296]{0:T(512)S(1)} %copy-done.8, s32[592]{0:T(1024)S(1)} %copy-done.6, s32[1]{0:T(128)} %get-tuple-element.13.total_ref, bf16[64,128,128]{2,1,0:T(8,128)(2,1)S(1)} %bitcast.71, bf16[32,128,128]{2,1,0:T(8,128)(2,1)S(1)} %get-tuple-element.23.right_ref, f32[64,128]{1,0:T(8,128)S(1)} %bitcast.76), custom_call_target="tpu_custom_call" | custom-call | tf_op jit(solution)/shard_map/pallas_call | solution.py:174
  92.5 9.7 %all-to-all-start.5 = ((f32[4,8,128]{2,1,0:T(8,128)}), f32[4,8,128]{2,1,0:T(8,128)S(1)}, u32[]{:S(2)}, u32[]{:S(2)}) async-start(f32[4,8,128]{2,1,0:T(8,128)} %bitcast.18), calls=%async_computation.5 | async-start | bytes 32768 | tf_op jit(solution)/shard_map/all_to_all | solution.py:213
  102.2 5.3 %all-to-all-done.5 = f32[4,8,128]{2,1,0:T(8,128)S(1)} async-done(((f32[4,8,128]{2,1,0:T(8,128)}), f32[4,8,128]{2,1,0:T(8,128)S(1)}, u32[]{:S(2)}, u32[]{:S(2)}) %all-to-all-start.5) | async-done | bytes 16416 | tf_op jit(solution)/shard_map/all_to_all | solution.py:213
  108.5 7.7 %all_to_all.102 = f32[4,8,128]{2,1,0:T(8,128)S(1)} all-to-all(f32[4,8,128]{2,1,0:T(8,128)S(1)} %bitcast.88), channel_id=1, replica_groups=mesh['src'=4,'grp'=32] {'src'}, dimensions={0} | all-to-all | bytes 32768 | tf_op jit(solution)/shard_map/all_to_all | solution.py:213
  116.2 1.6 copy-done.1
  117.8 1.2 copy-done.4
  119.0 3.7 %shard_map.98 = f32[64,128]{1,0:T(8,128)S(1)} custom-call(s32[320]{0:T(512)S(1)} %copy-done.9, s32[640]{0:T(1024)S(1)} %copy-done.7, s32[1]{0:T(128)} %get-tuple-element.10.total_ref, bf16[32,128,128]{2,1,0:T(8,128)(2,1)S(1)} %copy-done.4, bf16[64,128,128]{2,1,0:T(8,128)(2,1)S(1)} %copy-done.1, f32[32,128]{1,0:T(8,128)S(1)} %bitcast.81), custom_call_target="tpu_custom_call" | custom-call | tf_op jit(solution)/shard_map/pallas_call | solution.py:174
  122.7 11.2 %all_to_all.103 = f32[32,1,256]{2,1,0:T(1,128)S(1)} all-to-all(f32[32,1,256]{2,1,0:T(1,128)S(1)} %bitcast.77), channel_id=1, replica_groups=mesh['src'=4,'grp'=32] {'grp'}, dimensions={0} | all-to-all | bytes 65536 | tf_op jit(solution)/shard_map/all_to_all | solution.py:248
  134.0 0.8 add_subtract_fusion.1
  134.8 10.7 %all_to_all.104 = f32[32,1,256]{2,1,0:T(1,128)S(1)} all-to-all(f32[32,1,256]{2,1,0:T(1,128)S(1)} %broadcast_in_dim.78), channel_id=1, replica_groups=mesh['src'=4,'grp'=32] {'grp'}, dimensions={0} | all-to-all | bytes 65536 | tf_op jit(solution)/shard_map/all_to_all | solution.py:250
  145.6 3.8 %shard_map.99 = f32[32,128]{1,0:T(8,128)S(1)} custom-call(s32[296]{0:T(512)S(1)} %copy-done.8, s32[592]{0:T(1024)S(1)} %copy-done.6, s32[1]{0:T(128)} %get-tuple-element.13.total_ref, bf16[64,128,128]{2,1,0:T(8,128)(2,1)S(1)} %bitcast.72, bf16[32,128,128]{2,1,0:T(8,128)(2,1)S(1)} %get-tuple-element.23.right_ref, f32[64,128]{1,0:T(8,128)S(1)} %bitcast.78), custom_call_target="tpu_custom_call" | custom-call | tf_op jit(solution)/shard_map/pallas_call | solution.py:174
  149.4 16.4 %all_to_all.105 = f32[4,8,128]{2,1,0:T(8,128)S(1)} all-to-all(f32[4,8,128]{2,1,0:T(8,128)S(1)} %bitcast.82), channel_id=1, replica_groups=mesh['src'=4,'grp'=32] {'src'}, dimensions={0} | all-to-all | bytes 32768 | tf_op jit(solution)/shard_map/all_to_all | solution.py:213
  166.7 7.7 %all_to_all.106 = f32[4,8,128]{2,1,0:T(8,128)S(1)} all-to-all(f32[4,8,128]{2,1,0:T(8,128)S(1)} %bitcast.87), channel_id=1, replica_groups=mesh['src'=4,'grp'=32] {'src'}, dimensions={0} | all-to-all | bytes 32768 | tf_op jit(solution)/shard_map/all_to_all | solution.py:213
  174.4 1.6 copy-done.2
  176.0 1.2 copy-done.5
  177.2 3.7 %shard_map.100 = f32[64,128]{1,0:T(8,128)S(1)} custom-call(s32[320]{0:T(512)S(1)} %copy-done.9, s32[640]{0:T(1024)S(1)} %copy-done.7, s32[1]{0:T(128)} %get-tuple-element.10.total_ref, bf16[32,128,128]{2,1,0:T(8,128)(2,1)S(1)} %copy-done.5, bf16[64,128,128]{2,1,0:T(8,128)(2,1)S(1)} %copy-done.2, f32[32,128]{1,0:T(8,128)S(1)} %bitcast.80), custom_call_target="tpu_custom_call" | custom-call | tf_op jit(solution)/shard_map/pallas_call | solution.py:174
  180.9 10.4 %all_to_all.107 = f32[32,1,256]{2,1,0:T(1,128)S(1)} all-to-all(f32[32,1,256]{2,1,0:T(1,128)S(1)} %bitcast.75), channel_id=1, replica_groups=mesh['src'=4,'grp'=32] {'grp'}, dimensions={0} | all-to-all | bytes 65536 | tf_op jit(solution)/shard_map/all_to_all | solution.py:248
  191.5 0.8 add_subtract_fusion
  192.2 10.7 %all_to_all.108 = f32[32,1,256]{2,1,0:T(1,128)S(1)} all-to-all(f32[32,1,256]{2,1,0:T(1,128)S(1)} %broadcast_in_dim.80), channel_id=1, replica_groups=mesh['src'=4,'grp'=32] {'grp'}, dimensions={0} | all-to-all | bytes 65536 | tf_op jit(solution)/shard_map/all_to_all | solution.py:250
  203.0 4.4 %shard_map.101 = f32[32,128]{1,0:T(8,128)} custom-call(s32[296]{0:T(512)S(1)} %copy-done.8, s32[592]{0:T(1024)S(1)} %copy-done.6, s32[1]{0:T(128)} %get-tuple-element.13.total_ref, bf16[64,128,128]{2,1,0:T(8,128)(2,1)S(1)} %bitcast.73, bf16[32,128,128]{2,1,0:T(8,128)(2,1)S(1)} %get-tuple-element.23.right_ref, f32[64,128]{1,0:T(8,128)S(1)} %bitcast.74), custom_call_target="tpu_custom_call" | custom-call | tf_op jit(solution)/shard_map/pallas_call | solution.py:174
  207.4 11.8 %all-to-all-start.13 = ((f32[4,8,128]{2,1,0:T(8,128)}), f32[4,8,128]{2,1,0:T(8,128)S(1)}, u32[]{:S(2)}, u32[]{:S(2)}) async-start(f32[4,8,128]{2,1,0:T(8,128)} %bitcast.29), calls=%async_computation.13 | async-start | bytes 32768 | tf_op jit(solution)/shard_map/all_to_all | solution.py:213
  219.9 4.7 %all-to-all-done.13 = f32[4,8,128]{2,1,0:T(8,128)S(1)} async-done(((f32[4,8,128]{2,1,0:T(8,128)}), f32[4,8,128]{2,1,0:T(8,128)S(1)}, u32[]{:S(2)}, u32[]{:S(2)}) %all-to-all-start.13) | async-done | bytes 16416 | tf_op jit(solution)/shard_map/all_to_all | solution.py:213
  (59 shorter events, 5.0 us)
Async XLA Ops:
  0.6 15.4 %all-to-all-start = ((s32[4,1,8]{2,1,0:T(1,128)}), s32[4,1,8]{2,1,0:T(1,128)S(1)}, u32[]{:S(2)}, u32[]{:S(2)}) async-start(s32[4,1,8]{2,1,0:T(1,128)} %bitcast.91), calls=%async_computation | async-start | bytes 4096 | tf_op jit(solution)/shard_map/all_to_all | solution.py:213
  12.2 2.7 %copy-start.10 = (bf16[32,1,64,64]{3,2,0,1:T(8,128)(2,1)S(1)}, bf16[32,1,64,64]{3,2,0,1:T(8,128)(2,1)}, u32[]{:S(2)}) copy-start(bf16[32,1,64,64]{3,2,0,1:T(8,128)(2,1)} %copy.78) | copy-start | bytes 786436
  18.5 20.9 %all-to-all-start.1 = ((bf16[4,8,64,128]{3,2,1,0:T(8,128)(2,1)}), bf16[4,8,64,128]{3,2,1,0:T(8,128)(2,1)S(1)}, u32[]{:S(2)}, u32[]{:S(2)}) async-start(bf16[4,8,64,128]{3,2,1,0:T(8,128)(2,1)} %bitcast.6), calls=%async_computation.1 | async-start | bytes 1048576 | tf_op jit(solution)/shard_map/all_to_all | solution.py:213
  23.3 1.5 copy-start.15
  28.9 9.3 %copy-start.11 = (bf16[4096,64]{0,1:T(8,128)(2,1)S(1)}, bf16[4096,64]{0,1:T(8,128)(2,1)}, u32[]{:S(2)}) copy-start(bf16[4096,64]{0,1:T(8,128)(2,1)} %param.10) | copy-start | bytes 1572868
  28.9 9.4 %copy-start.14 = (f32[4096]{0:T(1024)S(1)}, f32[4096]{0:T(1024)}, u32[]{:S(2)}) copy-start(f32[4096]{0:T(1024)} %param.12) | copy-start | bytes 49156
  39.5 0.8 copy-start.12
  40.3 11.1 %all-to-all-start.2 = ((f32[4,8,128]{2,1,0:T(8,128)}), f32[4,8,128]{2,1,0:T(8,128)S(1)}, u32[]{:S(2)}, u32[]{:S(2)}) async-start(f32[4,8,128]{2,1,0:T(8,128)} %bitcast.14), calls=%async_computation.2 | async-start | bytes 32768 | tf_op jit(solution)/shard_map/all_to_all | solution.py:213
  47.4 4.0 %copy-start.7 = (s32[640]{0:T(1024)S(1)}, s32[640]{0:T(1024)}, u32[]{:S(2)}) copy-start(s32[640]{0:T(1024)} %get-tuple-element.9.right_ids) | copy-start | bytes 7684
  47.4 4.0 %copy-start.9 = (s32[320]{0:T(512)S(1)}, s32[320]{0:T(512)}, u32[]{:S(2)}) copy-start(s32[320]{0:T(512)} %get-tuple-element.8.left_ids) | copy-start | bytes 3844
  51.4 36.7 %copy-start.6 = (s32[592]{0:T(1024)S(1)}, s32[592]{0:T(1024)}, u32[]{:S(2)}) copy-start(s32[592]{0:T(1024)} %get-tuple-element.12.right_ids) | copy-start | bytes 7108
  51.4 36.7 %copy-start.8 = (s32[296]{0:T(512)S(1)}, s32[296]{0:T(512)}, u32[]{:S(2)}) copy-start(s32[296]{0:T(512)} %get-tuple-element.11.left_ids) | copy-start | bytes 3556
  51.4 1.6 copy-start
  53.0 1.2 copy-start.3
  58.6 49.3 %copy-start.13 = (f32[4096]{0:T(1024)S(1)}, f32[4096]{0:T(1024)}, u32[]{:S(2)}) copy-start(f32[4096]{0:T(1024)} %param.11) | copy-start | bytes 49156
  58.6 17.9 %all-to-all-start.3 = ((f32[32,1,256]{2,1,0:T(1,128)}), f32[32,1,256]{2,1,0:T(1,128)S(1)}, u32[]{:S(2)}, u32[]{:S(2)}) async-start(f32[32,1,256]{2,1,0:T(1,128)} %bitcast.16), calls=%async_computation.3 | async-start | bytes 65536 | tf_op jit(solution)/shard_map/all_to_all | solution.py:248
  92.5 15.0 %all-to-all-start.5 = ((f32[4,8,128]{2,1,0:T(8,128)}), f32[4,8,128]{2,1,0:T(8,128)S(1)}, u32[]{:S(2)}, u32[]{:S(2)}) async-start(f32[4,8,128]{2,1,0:T(8,128)} %bitcast.18), calls=%async_computation.5 | async-start | bytes 32768 | tf_op jit(solution)/shard_map/all_to_all | solution.py:213
  116.2 1.6 copy-start.1
  117.8 1.2 copy-start.4
  174.4 1.6 copy-start.2
  176.0 1.2 copy-start.5
  207.4 17.2 %all-to-all-start.13 = ((f32[4,8,128]{2,1,0:T(8,128)}), f32[4,8,128]{2,1,0:T(8,128)S(1)}, u32[]{:S(2)}, u32[]{:S(2)}) async-start(f32[4,8,128]{2,1,0:T(8,128)} %bitcast.29), calls=%async_computation.13 | async-start | bytes 32768 | tf_op jit(solution)/shard_map/all_to_all | solution.py:213
